TPU v7x, 32 devices: a whole 2x2x4 slice. The times are simulated.
32 devices in a mesh: blk: 8 (over z, y), pen: 4 (over x, core).
Axes of the slice: x: 2, y: 2, z: 4, core: 2. Of those that a mesh axis runs over, the one named last changes fastest.
Arguments:
- snapshots: bfloat16 [4, 512, 512, 128], P(None, ('blk', 'pen')), may hold values from -110 to 110
- start_time: float32 [128, 64], replicated, may hold values from -6 to 6
- start_plane: float32 [512, 32], replicated, may hold values from -6 to 6
Outputs:
- time_basis: float32 [128, 64], replicated
- plane_basis: float32 [512, 32], replicated
- core_tensor: bfloat16 [4, 32, 32768], P(None, None, ('blk', 'pen'))
All inputs are finite; a program needn't handle non-finite values.
Results may differ from a plain program's by a relative error of at most 0.005.
Values may be sent and summed in bfloat16 or wider, within the bound.
A program may use at most 64 MiB of HBM per device.

v0:
```python
import functools

import jax
import jax.numpy as jnp
from jax import lax
from jax.experimental import pallas as pl
from jax.experimental.pallas import tpu as pltpu
from jax.sharding import PartitionSpec as P

ITT = 3
ITX = 3
LANES = 128
BLOCK = 8

HIGHEST = lax.Precision.HIGHEST
MESH = pl.DeviceIdType.MESH


def product(left, right, contract):
    return lax.dot_general(
        left, right, ((contract[:1], contract[1:]), ((), ())),
        precision=HIGHEST, preferred_element_type=jnp.float32,
    )


def inverse_factor(square):
    size = square.shape[0]
    rows = lax.broadcasted_iota(jnp.int32, (size, size), 0)
    columns = lax.broadcasted_iota(jnp.int32, (size, size), 1)
    wide = jnp.concatenate([square, (rows == columns).astype(jnp.float32)], axis=1)
    shape = (BLOCK, 2 * size)
    sublane = lax.broadcasted_iota(jnp.int32, shape, 0)
    panels = [wide[first : first + BLOCK] for first in range(0, size, BLOCK)]
    done = []
    for number, panel in enumerate(panels):
        first = number * BLOCK
        spread = {
            (later, j): jnp.broadcast_to(panels[later][:, first + j : first + j + 1], shape)
            for later in range(number, len(panels))
            for j in range(BLOCK)
        }
        row = [jnp.broadcast_to(panel[j : j + 1], shape) for j in range(BLOCK)]
        entry = {
            (i, j): jnp.broadcast_to(spread[number, j][i : i + 1], shape)
            for i in range(BLOCK)
            for j in range(i + 1)
        }
        scale, inverse = [], {}
        for j in range(BLOCK):
            scale.append(lax.rsqrt(entry[j, j]))
            for i in range(j + 1, BLOCK):
                entry[i, j] = entry[i, j] * scale[j]
            for i in range(j + 1, BLOCK):
                for t in range(j + 1, i + 1):
                    entry[i, t] = entry[i, t] - entry[i, j] * entry[t, j]
        for j in range(BLOCK):
            inverse[j, j] = scale[j]
            for i in range(j + 1, BLOCK):
                total = entry[i, j] * inverse[j, j]
                for t in range(j + 1, i):
                    total = total + entry[i, t] * inverse[t, j]
                inverse[i, j] = -scale[i] * total
        solved = [
            sum(inverse[i, t] * row[t] for t in range(i + 1)) for i in range(BLOCK)
        ]
        if number + 1 < len(panels):
            twice = [
                sum(inverse[i, t] * solved[i] for i in range(t, BLOCK)) for t in range(BLOCK)
            ]
            for later in range(number + 1, len(panels)):
                panels[later] = panels[later] - sum(
                    spread[later, t] * twice[t] for t in range(BLOCK)
                )
        joined = solved[0]
        for i in range(1, BLOCK):
            joined = jnp.where(sublane == i, solved[i], joined)
        done.append(joined)
    return jnp.concatenate(done, axis=0)[:, size:]


def cholesky_round(rows):
    return product(inverse_factor(product(rows, rows, (1, 1))), rows, (1, 0))


def place(index):
    pens = lax.axis_size("pen")
    return (index // pens, lax.rem(index, pens))


def position():
    return lax.axis_index("blk") * lax.axis_size("pen") + lax.axis_index("pen")


def greet(count):
    me = position()
    barrier = pltpu.get_barrier_semaphore()

    def signal(step, carry):
        pl.semaphore_signal(
            barrier, inc=1, device_id=place(lax.rem(me + step, count)), device_id_type=MESH
        )
        return carry

    lax.fori_loop(1, count, signal, 0)
    pl.semaphore_wait(barrier, count - 1)


def sum_over_devices(count, parts, landed, gathered, sems):
    me = position()
    send_a, recv_a, send_b, recv_b = sems

    def scatter(step):
        there = lax.rem(me + step, count)
        return pltpu.make_async_remote_copy(
            src_ref=parts.at[there], dst_ref=landed.at[step],
            send_sem=send_a.at[step], recv_sem=recv_a.at[step],
            device_id=place(there), device_id_type=MESH,
        )

    def spread(step):
        there = lax.rem(me + step, count)
        return pltpu.make_async_remote_copy(
            src_ref=gathered.at[me], dst_ref=gathered.at[me],
            send_sem=send_b.at[step], recv_sem=recv_b.at[step],
            device_id=place(there), device_id_type=MESH,
        )

    def each(action):
        def body(step, carry):
            action(step)
            return carry

        lax.fori_loop(1, count, body, 0)

    each(lambda step: scatter(step).start())
    each(lambda step: scatter(step).wait())
    total = parts[me]
    for step in range(1, count):
        total = total + landed[step]
    gathered[me] = total
    each(lambda step: spread(step).start())
    each(lambda step: spread(step).wait())


def time_kernel(count, scale, share, start, basis, parts, landed, gathered, gram, *sems):
    depth = parts.shape[1]
    for piece in range(count):
        parts[piece] = share[piece * depth : (piece + 1) * depth, :]
    greet(count)
    sum_over_devices(count, parts, landed, gathered, sems)
    for piece in range(count):
        gram[piece * depth : (piece + 1) * depth, :] = gathered[piece] * scale
    basis[...] = start[...]

    def sweep(step, carry):
        basis[...] = cholesky_round(product(basis[...], gram[...], (1, 0)))
        return carry

    lax.fori_loop(0, ITT, sweep, 0)
    basis[...] = cholesky_round(basis[...])


def plane_kernel(count, scale, gram, start, basis, parts, landed, gathered, *sems):
    greet(count)
    rank, width = start.shape
    depth = parts.shape[2]
    basis[...] = start[...]

    def sweep(step, carry):
        share = product(basis[...], gram[...], (1, 0)) * scale
        stack = jnp.concatenate(
            [share[:, first : first + LANES] for first in range(0, width, LANES)], axis=0
        )
        for piece in range(count):
            parts[step, piece] = stack[piece * depth : (piece + 1) * depth]
        sum_over_devices(
            count, parts.at[step], landed.at[step], gathered.at[step],
            [sem.at[step] for sem in sems],
        )
        flat = jnp.concatenate([gathered[step, piece] for piece in range(count)], axis=0)
        total = jnp.concatenate(
            [flat[first : first + rank] for first in range(0, flat.shape[0], rank)], axis=1
        )
        basis[...] = cholesky_round(total)
        return carry

    lax.fori_loop(0, ITX, sweep, 0)
    basis[...] = cholesky_round(basis[...])


def in_vmem(number):
    return [pl.BlockSpec(memory_space=pltpu.VMEM)] * number


def time_subspace(share, start, scale, count):
    window = share.shape[0]
    depth = window // count
    slots = pltpu.VMEM((count, depth, window), jnp.float32)
    return pl.pallas_call(
        functools.partial(time_kernel, count, scale),
        out_shape=jax.ShapeDtypeStruct(start.shape, jnp.float32),
        in_specs=in_vmem(2),
        out_specs=pl.BlockSpec(memory_space=pltpu.VMEM),
        scratch_shapes=[slots, slots, slots, pltpu.VMEM((window, window), jnp.float32)]
        + [pltpu.SemaphoreType.DMA((count,))] * 4,
        compiler_params=pltpu.CompilerParams(
            collective_id=0, has_side_effects=True, vmem_limit_bytes=32 << 20
        ),
        cost_estimate=pl.CostEstimate(
            flops=60_000_000_000, bytes_accessed=100_000_000, transcendentals=0
        ),
    )(share, start)


def plane_subspace(share, start, scale, count):
    rank, width = start.shape
    depth = rank * width // LANES // count
    slots = pltpu.VMEM((ITX, count, depth, LANES), jnp.float32)
    return pl.pallas_call(
        functools.partial(plane_kernel, count, scale),
        out_shape=jax.ShapeDtypeStruct(start.shape, jnp.float32),
        in_specs=in_vmem(2),
        out_specs=pl.BlockSpec(memory_space=pltpu.VMEM),
        scratch_shapes=[slots] * 3 + [pltpu.SemaphoreType.DMA((ITX, count))] * 4,
        compiler_params=pltpu.CompilerParams(
            collective_id=1, has_side_effects=True, vmem_limit_bytes=32 << 20
        ),
    )(share, start)


def on_device(snapshots, start_time, start_plane):
    variables, planes, cell_count, window = snapshots.shape
    devices_all = lax.axis_size("blk") * lax.axis_size("pen")
    axes = ("blk", "pen")
    early = variables // 4
    early_cells = lax.all_to_all(
        snapshots[:early], axes, split_axis=2, concat_axis=1, tiled=True
    )
    row_matrix = snapshots.reshape(variables * planes * cell_count, window)
    partial_time = jnp.dot(row_matrix.T, row_matrix, preferred_element_type=jnp.float32)
    time_rows = time_subspace(
        partial_time,
        start_time.T,
        1.0 / float(variables * planes * cell_count * devices_all),
        devices_all,
    )
    time_basis = time_rows.T
    time_narrow = time_basis.astype(jnp.bfloat16)
    zero_block = jnp.zeros_like(time_narrow)
    pair_basis = jnp.stack(
        [
            jnp.concatenate([time_narrow, zero_block], axis=1),
            jnp.concatenate([zero_block, time_narrow], axis=1),
        ]
    )

    def truncate(cells):
        paired = cells.reshape(cells.shape[0], cells.shape[1], -1, 2, window)
        return jnp.einsum(
            "vxpqt,qtl->vxpl", paired, pair_basis, preferred_element_type=jnp.float32
        ).astype(jnp.bfloat16)

    pencils = [
        lax.all_to_all(
            truncate(snapshots[variable : variable + 1]),
            axes, split_axis=2, concat_axis=1, tiled=True,
        )
        for variable in range(early, variables)
    ]
    if early:
        pencils.insert(0, truncate(early_cells))
    column_total = float(variables * pencils[0].shape[2] * pencils[0].shape[3] * devices_all)
    partial_plane = sum(
        jnp.einsum("vxpl,vypl->xy", pencil, pencil, preferred_element_type=jnp.float32)
        for pencil in pencils
    )
    plane_rows = plane_subspace(partial_plane, start_plane.T, 1.0 / column_total, devices_all)
    plane_basis = plane_rows.T
    plane_narrow = plane_basis.astype(jnp.bfloat16)
    core_blocks = jnp.concatenate(
        [
            jnp.einsum("xk,vxpl->vkpl", plane_narrow, pencil, preferred_element_type=jnp.float32)
            for pencil in pencils
        ]
    ).astype(jnp.bfloat16)
    core_tensor = core_blocks.reshape(variables, core_blocks.shape[1], -1)
    return (time_basis, plane_basis, core_tensor)


def solution(mesh):
    return jax.shard_map(
        on_device,
        mesh=mesh,
        in_specs=(P(None, ("blk", "pen"), None, None), P(), P()),
        out_specs=(P(), P(), P(None, None, ("blk", "pen"))),
        check_vma=False,
    )
```

profile of v0, /device:TPU:0, one launch (start us, length us, event | category | flops | bytes accessed | tf_op | source)
XLA Modules:
  0.0 237.0 jit_solution(17297877424289198670)
XLA Ops:
  0.6 8.3 %convolution_bitcast_fusion.4.share = f32[128,128]{1,0:T(8,128)S(1)} fusion(bf16[4,16,512,128]{3,2,1,0:T(8,128)(2,1)} %param.3), kind=kOutput, calls=%fused_computation.29 | convolution fusion | flops 1073741824 | bytes 8454144 | tf_op jit(solution)/shard_map/dot_general | solution.py:240
  9.0 0.0 copy-start.1
  9.0 2.4 %fusion.33 = (bf16[1,16,512,128]{3,2,1,0:T(8,128)(2,1)S(1)}, bf16[1,16,512,128]{3,2,1,0:T(8,128)(2,1)S(1)}, bf16[1,16,512,128]{3,2,1,0:T(8,128)(2,1)}, bf16[1,16,512,128]{3,2,1,0:T(8,128)(2,1)}) fusion(bf16[4,16,512,128]{3,2,1,0:T(8,128)(2,1)S(1)} %copy-done.2), kind=kLoop, calls=%fused_computation.45 | loop fusion | bytes 16777216 | tf_op jit(solution)/shard_map/slice | solution.py:237
  11.4 28.6 %shard_map.58 = f32[64,128]{1,0:T(8,128)S(1)} custom-call(f32[128,128]{1,0:T(8,128)S(1)} %convolution_bitcast_fusion.4.share, f32[64,128]{1,0:T(8,128)S(1)} %bitcast.148), custom_call_target="tpu_custom_call" | custom-call | flops 60000002048 | bytes 100000000 | tf_op jit(solution)/shard_map/pallas_call | solution.py:199
  40.1 1.4 copy.70
  41.4 0.9 fusion.13
  42.3 1.8 copy.42
  44.1 3.4 %all-to-all-start.1 = ((bf16[1,16,256,128]{3,1,0,2:T(8,128)(2,1)}), bf16[1,16,256,128]{3,1,0,2:T(8,128)(2,1)}, u32[]{:S(2)}, u32[]{:S(2)}) async-start(bf16[1,16,256,128]{3,1,0,2:T(8,128)(2,1)} %copy.42), calls=%async_computation.1 | async-start | bytes 2097152 | tf_op jit(solution)/shard_map/all_to_all | solution.py:264
  47.5 2.9 %copy.71 = bf16[1,16,512,128]{3,1,2,0:T(8,128)(2,1)S(1)} copy(bf16[1,16,512,128]{3,2,1,0:T(8,128)(2,1)} %get-tuple-element.5) | data formatting | bytes 4194304
  50.5 0.9 fusion.16
  51.3 1.8 copy.47
  53.1 20.6 %all-to-all-done.1 = bf16[1,16,256,128]{3,1,0,2:T(8,128)(2,1)} async-done(((bf16[1,16,256,128]{3,1,0,2:T(8,128)(2,1)}), bf16[1,16,256,128]{3,1,0,2:T(8,128)(2,1)}, u32[]{:S(2)}, u32[]{:S(2)}) %all-to-all-start.1) | async-done | bytes 1048608 | tf_op jit(solution)/shard_map/all_to_all | solution.py:264
  73.7 3.9 %all-to-all-start.2 = ((bf16[1,16,256,128]{3,1,0,2:T(8,128)(2,1)}), bf16[1,16,256,128]{3,1,0,2:T(8,128)(2,1)}, u32[]{:S(2)}, u32[]{:S(2)}) async-start(bf16[1,16,256,128]{3,1,0,2:T(8,128)(2,1)} %copy.47), calls=%async_computation.2 | async-start | bytes 2097152 | tf_op jit(solution)/shard_map/all_to_all | solution.py:264
  77.6 2.9 %copy.72 = bf16[1,16,512,128]{3,1,2,0:T(8,128)(2,1)S(1)} copy(bf16[1,16,512,128]{3,2,1,0:T(8,128)(2,1)} %get-tuple-element.6) | data formatting | bytes 4194304
  80.5 0.9 fusion.19
  81.4 1.8 copy.52
  83.2 20.4 %all-to-all-done.2 = bf16[1,16,256,128]{3,1,0,2:T(8,128)(2,1)} async-done(((bf16[1,16,256,128]{3,1,0,2:T(8,128)(2,1)}), bf16[1,16,256,128]{3,1,0,2:T(8,128)(2,1)}, u32[]{:S(2)}, u32[]{:S(2)}) %all-to-all-start.2) | async-done | bytes 1048608 | tf_op jit(solution)/shard_map/all_to_all | solution.py:264
  103.6 3.6 %all-to-all-start.3 = ((bf16[1,16,256,128]{3,1,0,2:T(8,128)(2,1)}), bf16[1,16,256,128]{3,1,0,2:T(8,128)(2,1)S(1)}, u32[]{:S(2)}, u32[]{:S(2)}) async-start(bf16[1,16,256,128]{3,1,0,2:T(8,128)(2,1)} %copy.52), calls=%async_computation.3 | async-start | bytes 2097152 | tf_op jit(solution)/shard_map/all_to_all | solution.py:264
  107.2 2.7 %copy.69 = bf16[1,16,512,128]{3,1,0,2:T(8,128)(2,1)} copy(bf16[1,16,512,128]{3,2,1,0:T(8,128)(2,1)S(1)} %get-tuple-element.3) | data formatting | bytes 4194304
  109.9 23.6 %all-to-all-done.3 = bf16[1,16,256,128]{3,1,0,2:T(8,128)(2,1)S(1)} async-done(((bf16[1,16,256,128]{3,1,0,2:T(8,128)(2,1)}), bf16[1,16,256,128]{3,1,0,2:T(8,128)(2,1)S(1)}, u32[]{:S(2)}, u32[]{:S(2)}) %all-to-all-start.3) | async-done | bytes 1048608 | tf_op jit(solution)/shard_map/all_to_all | solution.py:264
  133.5 1.0 copy-done.5
  134.4 3.6 %all-to-all-start = ((bf16[1,16,512,128]{3,1,0,2:T(8,128)(2,1)}), bf16[1,16,512,128]{3,1,0,2:T(8,128)(2,1)S(1)}, u32[]{:S(2)}, u32[]{:S(2)}) async-start(bf16[1,16,512,128]{3,1,0,2:T(8,128)(2,1)} %copy.69), calls=%async_computation | async-start | bytes 4194304 | tf_op jit(solution)/shard_map/all_to_all | solution.py:236
  138.1 1.5 copy.104
  139.6 0.7 copy.44
  140.3 1.6 copy.103
  141.8 0.7 copy.49
  142.5 0.3 copy.102
  142.8 0.7 copy.54
  143.5 1.7 convolution_bitcast_fusion.2
  145.2 1.7 convolution_bitcast_fusion.1
  147.0 1.7 convolution_bitcast_fusion
  148.7 38.3 %all-to-all-done = bf16[1,16,512,128]{3,1,0,2:T(8,128)(2,1)S(1)} async-done(((bf16[1,16,512,128]{3,1,0,2:T(8,128)(2,1)}), bf16[1,16,512,128]{3,1,0,2:T(8,128)(2,1)S(1)}, u32[]{:S(2)}, u32[]{:S(2)}) %all-to-all-start) | async-done | bytes 2097184 | tf_op jit(solution)/shard_map/all_to_all | solution.py:236
  186.9 0.5 copy.37
  187.5 0.8 fusion.12
  188.3 0.4 copy-done.9
  188.7 0.3 copy-done.10
  189.0 0.3 copy-done.11
  189.4 0.8 fusion.24.gram
  190.2 0.0 copy-done
  190.2 43.5 %shard_map.59 = f32[32,512]{1,0:T(8,128)S(1)} custom-call(f32[512,512]{1,0:T(8,128)S(1)} %fusion.24.gram, f32[32,512]{1,0:T(8,128)S(1)} %bitcast.147), custom_call_target="tpu_custom_call" | custom-call | tf_op jit(solution)/shard_map/pallas_call | solution.py:219
  233.7 0.3 fusion.28
  234.0 0.0 copy-done.4
  234.0 0.3 fusion.27
  234.3 0.3 fusion.26
  234.6 0.4 fusion.25
  235.0 0.7 pad_maximum_fusion
  235.8 0.6 copy.107
  236.4 0.6 copy.108
  (22 shorter events, 0.1 us)
Async XLA Ops:
  0.6 8.3 %copy-start.2 = (bf16[4,16,512,128]{3,2,1,0:T(8,128)(2,1)S(1)}, bf16[4,16,512,128]{3,2,1,0:T(8,128)(2,1)}, u32[]{:S(2)}) copy-start(bf16[4,16,512,128]{3,2,1,0:T(8,128)(2,1)} %param.3) | copy-start | bytes 25165828
  9.0 2.4 %copy-start.1 = (f32[128,64]{0,1:T(8,128)S(1)}, f32[128,64]{0,1:T(8,128)}, u32[]{:S(2)}) copy-start(f32[128,64]{0,1:T(8,128)} %param.4) | copy-start | bytes 98308
  44.1 29.6 %all-to-all-start.1 = ((bf16[1,16,256,128]{3,1,0,2:T(8,128)(2,1)}), bf16[1,16,256,128]{3,1,0,2:T(8,128)(2,1)}, u32[]{:S(2)}, u32[]{:S(2)}) async-start(bf16[1,16,256,128]{3,1,0,2:T(8,128)(2,1)} %copy.42), calls=%async_computation.1 | async-start | bytes 2097152 | tf_op jit(solution)/shard_map/all_to_all | solution.py:264
  73.7 29.9 %all-to-all-start.2 = ((bf16[1,16,256,128]{3,1,0,2:T(8,128)(2,1)}), bf16[1,16,256,128]{3,1,0,2:T(8,128)(2,1)}, u32[]{:S(2)}, u32[]{:S(2)}) async-start(bf16[1,16,256,128]{3,1,0,2:T(8,128)(2,1)} %copy.47), calls=%async_computation.2 | async-start | bytes 2097152 | tf_op jit(solution)/shard_map/all_to_all | solution.py:264
  103.6 29.9 %all-to-all-start.3 = ((bf16[1,16,256,128]{3,1,0,2:T(8,128)(2,1)}), bf16[1,16,256,128]{3,1,0,2:T(8,128)(2,1)S(1)}, u32[]{:S(2)}, u32[]{:S(2)}) async-start(bf16[1,16,256,128]{3,1,0,2:T(8,128)(2,1)} %copy.52), calls=%async_computation.3 | async-start | bytes 2097152 | tf_op jit(solution)/shard_map/all_to_all | solution.py:264
  133.5 1.0 copy-start.5
  134.4 52.5 %all-to-all-start = ((bf16[1,16,512,128]{3,1,0,2:T(8,128)(2,1)}), bf16[1,16,512,128]{3,1,0,2:T(8,128)(2,1)S(1)}, u32[]{:S(2)}, u32[]{:S(2)}) async-start(bf16[1,16,512,128]{3,1,0,2:T(8,128)(2,1)} %copy.69), calls=%async_computation | async-start | bytes 4194304 | tf_op jit(solution)/shard_map/all_to_all | solution.py:236
  140.2 2.3 copy-start.6
  142.5 2.7 %copy-start.3 = (bf16[1,32,16,8,128]{4,2,1,3,0:T(8,128)(2,1)}, bf16[1,32,16,8,128]{4,2,1,3,0:T(8,128)(2,1)S(1)}, u32[]{:S(2)}) copy-start(bf16[1,32,16,8,128]{4,2,1,3,0:T(8,128)(2,1)S(1)} %copy.49) | copy-start | bytes 3145732
  143.5 3.4 %copy-start.7 = (bf16[1,32,16,8,128]{4,2,1,3,0:T(8,128)(2,1)}, bf16[1,32,16,8,128]{4,2,1,3,0:T(8,128)(2,1)S(1)}, u32[]{:S(2)}) copy-start(bf16[1,32,16,8,128]{4,2,1,3,0:T(8,128)(2,1)S(1)} %copy.54) | copy-start | bytes 3145732
  187.5 1.2 copy-start.9
  187.5 1.5 copy-start.10
  187.5 1.8 copy-start.11
  189.4 0.8 copy-start
  189.4 44.3 %copy-start.8 = (bf16[1,32,16,8,128]{4,2,1,3,0:T(8,128)(2,1)S(1)}, bf16[1,32,16,8,128]{4,2,1,3,0:T(8,128)(2,1)}, u32[]{:S(2)}) copy-start(bf16[1,32,16,8,128]{4,2,1,3,0:T(8,128)(2,1)} %copy-done.7) | copy-start | bytes 3145732
  190.1 43.8 %copy-start.4 = (bf16[1,32,16,8,128]{4,2,1,3,0:T(8,128)(2,1)S(1)}, bf16[1,32,16,8,128]{4,2,1,3,0:T(8,128)(2,1)}, u32[]{:S(2)}) copy-start(bf16[1,32,16,8,128]{4,2,1,3,0:T(8,128)(2,1)} %copy-done.3) | copy-start | bytes 3145732
where the time goes:
time: 238 us; the launch traced here: 237 us
  waiting for transfers between devices  103 us (43%)
  Pallas kernels  72.1 us (30%)
  local copies, waits for them, and re-layouts  27 us (11%)
  matrix products  19 us (8%)
  starting transfers between devices  14.5 us (6%)
    all_to_all x3, waiting for transfers between devices, on_device(): lax.all_to_all(truncate(snapshots[variable:variable + 1]), axes, split_ax...  64.5 us
    pallas_call x1, Pallas kernels, plane_subspace(): pl.pallas_call(functools.partial(plane_kernel, count, scale), out_shape=j...  43.5 us
    all_to_all x1, waiting for transfers between devices, on_device(): lax.all_to_all(snapshots[:early], axes, split_axis=2, concat_axis=1, tile...  38.3 us
    pallas_call x1, Pallas kernels, time_subspace(): pl.pallas_call(functools.partial(time_kernel, count, scale), out_shape=ja...  28.6 us
    unnamed x30, local copies, waits for them, and re-layouts  13.2 us
    all_to_all x3, starting transfers between devices, on_device(): lax.all_to_all(truncate(snapshots[variable:variable + 1]), axes, split_ax...  10.8 us
    dot_general x1, matrix products, on_device(): jnp.dot(row_matrix.T, row_matrix, preferred_element_type=jnp.float32)  8.31 us
    dot_general x4, matrix products, on_device(): jnp.einsum('vxpl,vypl->xy', pencil, pencil, preferred_element_type=jnp.fl...  5.93 us
  transfers between devices with their start and end apart: 4, of which 4 were waited for; matrix products, arithmetic and copies ran while one was open for 10% of the time, Pallas kernels for 0%

commit v1 on v0

--- a/solution.py
+++ b/solution.py
@@ -206,9 +206,6 @@
         compiler_params=pltpu.CompilerParams(
             collective_id=0, has_side_effects=True, vmem_limit_bytes=32 << 20
         ),
-        cost_estimate=pl.CostEstimate(
-            flops=60_000_000_000, bytes_accessed=100_000_000, transcendentals=0
-        ),
     )(share, start)
 
 
@@ -228,14 +225,70 @@
     )(share, start)
 
 
+def exchange_kernel(count, snapshots, wide, pencils, parts, send, recv):
+    greet(count)
+    me = position()
+    variables, planes, cells, window = snapshots.shape
+    own = cells // count
+    half = own // 2
+    blocks = variables * planes
+
+    def truncated(owner):
+        here = pl.ds(pl.multiple_of(owner * own, own), own)
+        rows = snapshots[:, :, here, :].reshape(blocks * own, window)
+        pair = jnp.dot(rows, wide[...], preferred_element_type=jnp.float32)
+        pair = pair.reshape(blocks, own, pair.shape[1])
+        lanes = pair.shape[2] // 2
+        packed = pair[:, :half, :lanes] + pair[:, half:, lanes:]
+        return packed.reshape(blocks * half, lanes).astype(jnp.bfloat16)
+
+    def copy(step):
+        there = lax.rem(me + step, count)
+        return pltpu.make_async_remote_copy(
+            src_ref=parts.at[there], dst_ref=pencils.at[me],
+            send_sem=send.at[step], recv_sem=recv.at[step],
+            device_id=place(there), device_id_type=MESH,
+        )
+
+    def begin(step, carry):
+        there = lax.rem(me + step, count)
+        parts[there] = truncated(there)
+        copy(step).start()
+        return carry
+
+    def finish(step, carry):
+        copy(step).wait()
+        return carry
+
+    lax.fori_loop(1, count, begin, 0)
+    pencils[me] = truncated(me)
+    lax.fori_loop(1, count, finish, 0)
+
+
+def exchange(snapshots, narrow, count):
+    variables, planes, cells, window = snapshots.shape
+    zero = jnp.zeros_like(narrow)
+    wide = jnp.concatenate([narrow, zero, zero, narrow], axis=1)
+    half = cells // count // 2
+    shape = (count, variables * planes * half, 2 * narrow.shape[1])
+    pencils = pl.pallas_call(
+        functools.partial(exchange_kernel, count),
+        out_shape=jax.ShapeDtypeStruct(shape, jnp.bfloat16),
+        in_specs=in_vmem(2),
+        out_specs=pl.BlockSpec(memory_space=pltpu.VMEM),
+        scratch_shapes=[pltpu.VMEM(shape, jnp.bfloat16)]
+        + [pltpu.SemaphoreType.DMA((count,))] * 2,
+        compiler_params=pltpu.CompilerParams(
+            collective_id=2, has_side_effects=True, vmem_limit_bytes=40 << 20
+        ),
+    )(snapshots, wide)
+    pencils = pencils.reshape(count, variables, planes, half, shape[2])
+    return pencils.transpose(1, 0, 2, 3, 4).reshape(variables, count * planes, half, shape[2])
+
+
 def on_device(snapshots, start_time, start_plane):
     variables, planes, cell_count, window = snapshots.shape
     devices_all = lax.axis_size("blk") * lax.axis_size("pen")
-    axes = ("blk", "pen")
-    early = variables // 4
-    early_cells = lax.all_to_all(
-        snapshots[:early], axes, split_axis=2, concat_axis=1, tiled=True
-    )
     row_matrix = snapshots.reshape(variables * planes * cell_count, window)
     partial_time = jnp.dot(row_matrix.T, row_matrix, preferred_element_type=jnp.float32)
     time_rows = time_subspace(
@@ -246,44 +299,20 @@
     )
     time_basis = time_rows.T
     time_narrow = time_basis.astype(jnp.bfloat16)
-    zero_block = jnp.zeros_like(time_narrow)
-    pair_basis = jnp.stack(
-        [
-            jnp.concatenate([time_narrow, zero_block], axis=1),
-            jnp.concatenate([zero_block, time_narrow], axis=1),
-        ]
-    )
-
-    def truncate(cells):
-        paired = cells.reshape(cells.shape[0], cells.shape[1], -1, 2, window)
-        return jnp.einsum(
-            "vxpqt,qtl->vxpl", paired, pair_basis, preferred_element_type=jnp.float32
-        ).astype(jnp.bfloat16)
-
-    pencils = [
-        lax.all_to_all(
-            truncate(snapshots[variable : variable + 1]),
-            axes, split_axis=2, concat_axis=1, tiled=True,
-        )
-        for variable in range(early, variables)
-    ]
-    if early:
-        pencils.insert(0, truncate(early_cells))
-    column_total = float(variables * pencils[0].shape[2] * pencils[0].shape[3] * devices_all)
-    partial_plane = sum(
-        jnp.einsum("vxpl,vypl->xy", pencil, pencil, preferred_element_type=jnp.float32)
-        for pencil in pencils
+    pencils = exchange(snapshots, time_narrow, devices_all)
+    column_total = float(variables * pencils.shape[2] * pencils.shape[3] * devices_all)
+    partial_plane = jnp.einsum(
+        "vxpl,vypl->xy", pencils, pencils, preferred_element_type=jnp.float32
     )
     plane_rows = plane_subspace(partial_plane, start_plane.T, 1.0 / column_total, devices_all)
     plane_basis = plane_rows.T
     plane_narrow = plane_basis.astype(jnp.bfloat16)
-    core_blocks = jnp.concatenate(
-        [
-            jnp.einsum("xk,vxpl->vkpl", plane_narrow, pencil, preferred_element_type=jnp.float32)
-            for pencil in pencils
-        ]
+    core_blocks = jnp.einsum(
+        "xk,vxpl->vkpl", plane_narrow, pencils, preferred_element_type=jnp.float32
     ).astype(jnp.bfloat16)
-    core_tensor = core_blocks.reshape(variables, core_blocks.shape[1], -1)
+    rank = plane_narrow.shape[1]
+    core_blocks = core_blocks.reshape(variables, rank, pencils.shape[2], 2, -1)
+    core_tensor = core_blocks.transpose(0, 1, 3, 2, 4).reshape(variables, rank, -1)
     return (time_basis, plane_basis, core_tensor)
 
 

time: 238 us -> 204 us (0.86)
  Pallas kernels: 72.1 us -> 184 us
  waiting for transfers between devices: 103 us -> 0 us
  local copies, waits for them, and re-layouts: 27 us -> 7.7 us
  starting transfers between devices: 14.5 us -> 0 us
  matrix products: 19 us -> 11.3 us
    all_to_all x4 -> x0, waiting for transfers between devices: 103 us -> none  [the longest x3 64.5 us: on_device(): lax.all_to_all(truncate(snapshots[variable:variable + 1]), axes, split_ax...]
    pallas_call x0 -> x1, Pallas kernels: none -> 83.7 us  [exchange(): pl.pallas_call(functools.partial(exchange_kernel, count), out_shape=jax.S...]
    pallas_call x1, Pallas kernels: 43.5 us -> 71.8 us  [plane_subspace(): pl.pallas_call(functools.partial(plane_kernel, count, scale), out_shape=j...]
    all_to_all x4 -> x0, starting transfers between devices: 14.5 us -> none  [the longest x3 10.8 us: on_device(): lax.all_to_all(truncate(snapshots[variable:variable + 1]), axes, split_ax...]
    unnamed x30 -> x8, local copies, waits for them, and re-layouts: 13.2 us -> 4.63 us
    dot_general x12 -> x2, matrix products: 10.6 us -> 3.17 us  [the longest x1 2.35 us: on_device(): jnp.einsum('vxpl,vypl->xy', pencils, pencils, preferred_element_type=jnp....]
    all_to_all x7 -> x0, local copies, waits for them, and re-layouts: 5.93 us -> none  [the longest x6 5.39 us: on_device(): lax.all_to_all(truncate(snapshots[variable:variable + 1]), axes, split_ax...]
    convert_element_type x3 -> x0, local copies, waits for them, and re-layouts: 5.42 us -> none  [truncate(): return jnp.einsum('vxpqt,qtl->vxpl', paired, pair_basis, preferred_elemen...]
  transfers between devices with their start and end apart: 4 -> 0, of which waited for: 4 -> 0; matrix products, arithmetic and copies ran while one was open for 10% -> 0% of each run, Pallas kernels for 0% -> 0%
where the time goes in v1:
time: 204 us
  Pallas kernels  184 us (90%)
  matrix products  11.3 us (6%)
  local copies, waits for them, and re-layouts  7.7 us (4%)
    pallas_call x1, Pallas kernels, exchange(): pl.pallas_call(functools.partial(exchange_kernel, count), out_shape=jax.S...  83.7 us
    pallas_call x1, Pallas kernels, plane_subspace(): pl.pallas_call(functools.partial(plane_kernel, count, scale), out_shape=j...  71.8 us
    pallas_call x1, Pallas kernels, time_subspace(): pl.pallas_call(functools.partial(time_kernel, count, scale), out_shape=ja...  28.8 us
    dot_general x1, matrix products, on_device(): jnp.dot(row_matrix.T, row_matrix, preferred_element_type=jnp.float32)  8.16 us
    unnamed x8, local copies, waits for them, and re-layouts  4.63 us

profile of v1, /device:TPU:0, one launch (start us, length us, event | category | flops | bytes accessed | tf_op | source)
XLA Modules:
  0.0 204.2 jit_solution(16841571817510994801)
XLA Ops:
  0.6 0.1 pad.1.clone
  0.7 0.0 copy-start.2
  0.7 8.2 %convolution_bitcast_fusion.share = f32[128,128]{1,0:T(8,128)S(1)} fusion(bf16[4,16,512,128]{3,2,1,0:T(8,128)(2,1)} %snapshots.1), kind=kOutput, calls=%fused_computation.5 | convolution fusion | flops 1073741824 | bytes 8454144 | tf_op jit(solution)/shard_map/dot_general | solution.py:293
  8.9 0.0 copy-done.2
  8.9 28.8 %shard_map.58 = f32[64,128]{1,0:T(8,128)S(1)} custom-call(f32[128,128]{1,0:T(8,128)S(1)} %convolution_bitcast_fusion.share, f32[64,128]{1,0:T(8,128)S(1)} %bitcast.41), custom_call_target="tpu_custom_call" | custom-call | tf_op jit(solution)/shard_map/pallas_call | solution.py:199
  37.7 0.1 copy.7
  37.9 0.1 pad_maximum_fusion.wide
  38.0 0.0 copy-start
  38.0 3.4 %copy-done = bf16[4,16,512,128]{3,2,1,0:T(8,128)(2,1)S(1)} copy-done((bf16[4,16,512,128]{3,2,1,0:T(8,128)(2,1)S(1)}, bf16[4,16,512,128]{3,2,1,0:T(8,128)(2,1)}, u32[]{:S(2)}) %copy-start) | copy-done | bytes 8388632
  41.3 83.7 %shard_map.59 = bf16[32,512,128]{2,1,0:T(8,128)(2,1)S(1)} custom-call(bf16[4,16,512,128]{3,2,1,0:T(8,128)(2,1)S(1)} %copy-done, bf16[128,256]{1,0:T(8,128)(2,1)S(1)} %pad_maximum_fusion.wide), custom_call_target="tpu_custom_call" | custom-call | tf_op jit(solution)/shard_map/pallas_call | solution.py:274
  125.0 1.0 copy.8
  126.0 0.0 copy-start.1
  126.0 2.4 %fusion.2.gram = f32[512,512]{1,0:T(8,128)S(1)} fusion(bf16[4,512,8,128]{3,1,2,0:T(8,128)(2,1)S(1)} %bitcast.42), kind=kOutput, calls=%fused_computation.2 | convolution fusion | flops 2147483648 | bytes 5242880 | tf_op jit(solution)/shard_map/vxpl,vypl->xy/dot_general | solution.py:304
  128.4 0.0 copy-done.1
  128.4 71.8 %shard_map.60 = f32[32,512]{1,0:T(8,128)S(1)} custom-call(f32[512,512]{1,0:T(8,128)S(1)} %fusion.2.gram, f32[32,512]{1,0:T(8,128)S(1)} %bitcast.40), custom_call_target="tpu_custom_call" | custom-call | tf_op jit(solution)/shard_map/pallas_call | solution.py:216
  200.2 0.8 fusion.5
  201.0 0.3 reshape.21
  201.3 0.6 copy.11
  201.9 1.1 reshape.22
  202.9 0.6 copy.24
  203.5 0.6 copy.25
  (1 shorter events, 0.0 us)
Async XLA Ops:
  0.7 8.2 %copy-start.2 = (f32[128,64]{0,1:T(8,128)S(1)}, f32[128,64]{0,1:T(8,128)}, u32[]{:S(2)}) copy-start(f32[128,64]{0,1:T(8,128)} %param.4) | copy-start | bytes 98308
  38.0 3.4 %copy-start = (bf16[4,16,512,128]{3,2,1,0:T(8,128)(2,1)S(1)}, bf16[4,16,512,128]{3,2,1,0:T(8,128)(2,1)}, u32[]{:S(2)}) copy-start(bf16[4,16,512,128]{3,2,1,0:T(8,128)(2,1)} %snapshots.1) | copy-start | bytes 25165828
  126.0 2.4 %copy-start.1 = (f32[512,32]{0,1:T(8,128)S(1)}, f32[512,32]{0,1:T(8,128)}, u32[]{:S(2)}) copy-start(f32[512,32]{0,1:T(8,128)} %param.5) | copy-start | bytes 196612

commit v2 on v1

--- a/solution.py
+++ b/solution.py
@@ -242,8 +242,14 @@
         packed = pair[:, :half, :lanes] + pair[:, half:, lanes:]
         return packed.reshape(blocks * half, lanes).astype(jnp.bfloat16)
 
+    side = count // 2
+
+    def partner(step):
+        far = lax.rem(me // side + 1 - step // side, 2)
+        return far * side + lax.rem(me + step, side)
+
     def copy(step):
-        there = lax.rem(me + step, count)
+        there = partner(step)
         return pltpu.make_async_remote_copy(
             src_ref=parts.at[there], dst_ref=pencils.at[me],
             send_sem=send.at[step], recv_sem=recv.at[step],
@@ -251,7 +257,7 @@
         )
 
     def begin(step, carry):
-        there = lax.rem(me + step, count)
+        there = partner(step)
         parts[there] = truncated(there)
         copy(step).start()
         return carry
@@ -260,9 +266,11 @@
         copy(step).wait()
         return carry
 
-    lax.fori_loop(1, count, begin, 0)
+    lax.fori_loop(0, side, begin, 0)
+    lax.fori_loop(side + 1, count, begin, 0)
     pencils[me] = truncated(me)
-    lax.fori_loop(1, count, finish, 0)
+    lax.fori_loop(0, side, finish, 0)
+    lax.fori_loop(side + 1, count, finish, 0)
 
 
 def exchange(snapshots, narrow, count):

time: 204 us -> 207 us (1.015)
  Pallas kernels: 184 us -> 187 us
    pallas_call x1, Pallas kernels: 83.7 us -> 105 us  [exchange(): pl.pallas_call(functools.partial(exchange_kernel, count), out_shape=jax.S...]
    pallas_call x1, Pallas kernels: 71.8 us -> 53.5 us  [plane_subspace(): pl.pallas_call(functools.partial(plane_kernel, count, scale), out_shape=j...]
where the time goes in v2:
time: 207 us
  Pallas kernels  187 us (90%)
  matrix products  11.3 us (5%)
  local copies, waits for them, and re-layouts  7.71 us (4%)
    pallas_call x1, Pallas kernels, exchange(): pl.pallas_call(functools.partial(exchange_kernel, count), out_shape=jax.S...  105 us
    pallas_call x1, Pallas kernels, plane_subspace(): pl.pallas_call(functools.partial(plane_kernel, count, scale), out_shape=j...  53.5 us
    pallas_call x1, Pallas kernels, time_subspace(): pl.pallas_call(functools.partial(time_kernel, count, scale), out_shape=ja...  28.8 us
    dot_general x1, matrix products, on_device(): jnp.dot(row_matrix.T, row_matrix, preferred_element_type=jnp.float32)  8.16 us
    unnamed x8, local copies, waits for them, and re-layouts  4.63 us

profile of v2, /device:TPU:0, one launch (start us, length us, event | category | flops | bytes accessed | tf_op | source)
XLA Modules:
  0.0 207.3 jit_solution(9522989567352665556)
XLA Ops:
  0.6 0.1 pad.1.clone
  0.7 0.0 copy-start.2
  0.7 8.2 %convolution_bitcast_fusion.share = f32[128,128]{1,0:T(8,128)S(1)} fusion(bf16[4,16,512,128]{3,2,1,0:T(8,128)(2,1)} %snapshots.1), kind=kOutput, calls=%fused_computation.5 | convolution fusion | flops 1073741824 | bytes 8454144 | tf_op jit(solution)/shard_map/dot_general | solution.py:301
  8.9 0.0 copy-done.2
  8.9 28.8 %shard_map.58 = f32[64,128]{1,0:T(8,128)S(1)} custom-call(f32[128,128]{1,0:T(8,128)S(1)} %convolution_bitcast_fusion.share, f32[64,128]{1,0:T(8,128)S(1)} %bitcast.41), custom_call_target="tpu_custom_call" | custom-call | tf_op jit(solution)/shard_map/pallas_call | solution.py:199
  37.7 0.1 copy.7
  37.9 0.1 pad_maximum_fusion.wide
  38.0 0.0 copy-start
  38.0 3.4 %copy-done = bf16[4,16,512,128]{3,2,1,0:T(8,128)(2,1)S(1)} copy-done((bf16[4,16,512,128]{3,2,1,0:T(8,128)(2,1)S(1)}, bf16[4,16,512,128]{3,2,1,0:T(8,128)(2,1)}, u32[]{:S(2)}) %copy-start) | copy-done | bytes 8388632
  41.3 105.1 %shard_map.59 = bf16[32,512,128]{2,1,0:T(8,128)(2,1)S(1)} custom-call(bf16[4,16,512,128]{3,2,1,0:T(8,128)(2,1)S(1)} %copy-done, bf16[128,256]{1,0:T(8,128)(2,1)S(1)} %pad_maximum_fusion.wide), custom_call_target="tpu_custom_call" | custom-call | tf_op jit(solution)/shard_map/pallas_call | solution.py:282
  146.4 1.0 copy.8
  147.4 0.0 copy-start.1
  147.4 2.4 %fusion.2.gram = f32[512,512]{1,0:T(8,128)S(1)} fusion(bf16[4,512,8,128]{3,1,2,0:T(8,128)(2,1)S(1)} %bitcast.42), kind=kOutput, calls=%fused_computation.2 | convolution fusion | flops 2147483648 | bytes 5242880 | tf_op jit(solution)/shard_map/vxpl,vypl->xy/dot_general | solution.py:312
  149.8 0.0 copy-done.1
  149.8 53.5 %shard_map.60 = f32[32,512]{1,0:T(8,128)S(1)} custom-call(f32[512,512]{1,0:T(8,128)S(1)} %fusion.2.gram, f32[32,512]{1,0:T(8,128)S(1)} %bitcast.40), custom_call_target="tpu_custom_call" | custom-call | tf_op jit(solution)/shard_map/pallas_call | solution.py:216
  203.3 0.8 fusion.5
  204.1 0.3 reshape.21
  204.4 0.6 copy.11
  205.0 1.1 reshape.22
  206.0 0.6 copy.24
  206.6 0.6 copy.25
  (1 shorter events, 0.0 us)
Async XLA Ops:
  0.7 8.2 %copy-start.2 = (f32[128,64]{0,1:T(8,128)S(1)}, f32[128,64]{0,1:T(8,128)}, u32[]{:S(2)}) copy-start(f32[128,64]{0,1:T(8,128)} %param.4) | copy-start | bytes 98308
  38.0 3.4 %copy-start = (bf16[4,16,512,128]{3,2,1,0:T(8,128)(2,1)S(1)}, bf16[4,16,512,128]{3,2,1,0:T(8,128)(2,1)}, u32[]{:S(2)}) copy-start(bf16[4,16,512,128]{3,2,1,0:T(8,128)(2,1)} %snapshots.1) | copy-start | bytes 25165828
  147.4 2.4 %copy-start.1 = (f32[512,32]{0,1:T(8,128)S(1)}, f32[512,32]{0,1:T(8,128)}, u32[]{:S(2)}) copy-start(f32[512,32]{0,1:T(8,128)} %param.5) | copy-start | bytes 196612

commit v3 on v2

--- a/solution.py
+++ b/solution.py
@@ -266,8 +266,11 @@
         copy(step).wait()
         return carry
 
-    lax.fori_loop(0, side, begin, 0)
-    lax.fori_loop(side + 1, count, begin, 0)
+    def begin_two(step, carry):
+        return begin(side + 1 + step, begin(step, carry))
+
+    lax.fori_loop(0, side - 1, begin_two, 0)
+    begin(side - 1, 0)
     pencils[me] = truncated(me)
     lax.fori_loop(0, side, finish, 0)
     lax.fori_loop(side + 1, count, finish, 0)

time: 207 us -> 192 us (0.928)
  Pallas kernels: 187 us -> 172 us
    pallas_call x1, Pallas kernels: 53.5 us -> 42.4 us  [plane_subspace(): pl.pallas_call(functools.partial(plane_kernel, count, scale), out_shape=j...]
    pallas_call x1, Pallas kernels: 105 us -> 101 us  [exchange(): pl.pallas_call(functools.partial(exchange_kernel, count), out_shape=jax.S...]
where the time goes in v3:
time: 192 us
  Pallas kernels  172 us (90%)
  matrix products  11.3 us (6%)
  local copies, waits for them, and re-layouts  7.7 us (4%)
    pallas_call x1, Pallas kernels, exchange(): pl.pallas_call(functools.partial(exchange_kernel, count), out_shape=jax.S...  101 us
    pallas_call x1, Pallas kernels, plane_subspace(): pl.pallas_call(functools.partial(plane_kernel, count, scale), out_shape=j...  42.4 us
    pallas_call x1, Pallas kernels, time_subspace(): pl.pallas_call(functools.partial(time_kernel, count, scale), out_shape=ja...  28.8 us
    dot_general x1, matrix products, on_device(): jnp.dot(row_matrix.T, row_matrix, preferred_element_type=jnp.float32)  8.16 us
    unnamed x8, local copies, waits for them, and re-layouts  4.63 us

profile of v3, /device:TPU:0, one launch (start us, length us, event | category | flops | bytes accessed | tf_op | source)
XLA Modules:
  0.0 191.8 jit_solution(4679020820061620009)
XLA Ops:
  0.6 0.1 pad.1.clone
  0.7 0.0 copy-start.2
  0.7 8.2 %convolution_bitcast_fusion.share = f32[128,128]{1,0:T(8,128)S(1)} fusion(bf16[4,16,512,128]{3,2,1,0:T(8,128)(2,1)} %snapshots.1), kind=kOutput, calls=%fused_computation.5 | convolution fusion | flops 1073741824 | bytes 8454144 | tf_op jit(solution)/shard_map/dot_general | solution.py:304
  8.9 0.0 copy-done.2
  8.9 28.8 %shard_map.58 = f32[64,128]{1,0:T(8,128)S(1)} custom-call(f32[128,128]{1,0:T(8,128)S(1)} %convolution_bitcast_fusion.share, f32[64,128]{1,0:T(8,128)S(1)} %bitcast.41), custom_call_target="tpu_custom_call" | custom-call | tf_op jit(solution)/shard_map/pallas_call | solution.py:199
  37.7 0.1 copy.7
  37.9 0.1 pad_maximum_fusion.wide
  38.0 0.0 copy-start
  38.0 3.4 %copy-done = bf16[4,16,512,128]{3,2,1,0:T(8,128)(2,1)S(1)} copy-done((bf16[4,16,512,128]{3,2,1,0:T(8,128)(2,1)S(1)}, bf16[4,16,512,128]{3,2,1,0:T(8,128)(2,1)}, u32[]{:S(2)}) %copy-start) | copy-done | bytes 8388632
  41.3 100.7 %shard_map.59 = bf16[32,512,128]{2,1,0:T(8,128)(2,1)S(1)} custom-call(bf16[4,16,512,128]{3,2,1,0:T(8,128)(2,1)S(1)} %copy-done, bf16[128,256]{1,0:T(8,128)(2,1)S(1)} %pad_maximum_fusion.wide), custom_call_target="tpu_custom_call" | custom-call | tf_op jit(solution)/shard_map/pallas_call | solution.py:285
  142.1 1.0 copy.8
  143.0 0.0 copy-start.1
  143.0 2.4 %fusion.2.gram = f32[512,512]{1,0:T(8,128)S(1)} fusion(bf16[4,512,8,128]{3,1,2,0:T(8,128)(2,1)S(1)} %bitcast.42), kind=kOutput, calls=%fused_computation.2 | convolution fusion | flops 2147483648 | bytes 5242880 | tf_op jit(solution)/shard_map/vxpl,vypl->xy/dot_general | solution.py:315
  145.4 0.0 copy-done.1
  145.4 42.4 %shard_map.60 = f32[32,512]{1,0:T(8,128)S(1)} custom-call(f32[512,512]{1,0:T(8,128)S(1)} %fusion.2.gram, f32[32,512]{1,0:T(8,128)S(1)} %bitcast.40), custom_call_target="tpu_custom_call" | custom-call | tf_op jit(solution)/shard_map/pallas_call | solution.py:216
  187.9 0.8 fusion.5
  188.7 0.3 reshape.21
  188.9 0.6 copy.11
  189.6 1.1 reshape.22
  190.6 0.6 copy.24
  191.2 0.6 copy.25
  (1 shorter events, 0.0 us)
Async XLA Ops:
  0.7 8.2 %copy-start.2 = (f32[128,64]{0,1:T(8,128)S(1)}, f32[128,64]{0,1:T(8,128)}, u32[]{:S(2)}) copy-start(f32[128,64]{0,1:T(8,128)} %param.4) | copy-start | bytes 98308
  38.0 3.4 %copy-start = (bf16[4,16,512,128]{3,2,1,0:T(8,128)(2,1)S(1)}, bf16[4,16,512,128]{3,2,1,0:T(8,128)(2,1)}, u32[]{:S(2)}) copy-start(bf16[4,16,512,128]{3,2,1,0:T(8,128)(2,1)} %snapshots.1) | copy-start | bytes 25165828
  143.0 2.4 %copy-start.1 = (f32[512,32]{0,1:T(8,128)S(1)}, f32[512,32]{0,1:T(8,128)}, u32[]{:S(2)}) copy-start(f32[512,32]{0,1:T(8,128)} %param.5) | copy-start | bytes 196612
